TPU v7x, 256 devices: a whole 4x4x8 slice. The times are simulated.
256 devices in a mesh: gx: 8 (over z), gy: 8 (over y_lo, x), gz: 4 (over y_hi, core).
Axes of the slice: x: 4, y: 4 (y_hi: 2, y_lo: 2; y = y_hi * 2 + y_lo), z: 8, core: 2. Of those that a mesh axis runs over, the one named last changes fastest.
Arguments:
- saved_inputs: bfloat16 [1024, 12288], P('gx', 'gy'), may hold values from -6 to 6
- w_first: bfloat16 [12288, 24576], P('gy', ('gx', 'gz')), may hold values from -0.0546875 to 0.0546875
- w_second: bfloat16 [24576, 12288], P(('gx', 'gz'), 'gy'), may hold values from -0.0390625 to 0.0390625
- grad_output: bfloat16 [1024, 12288], P('gx', 'gy'), may hold values from -3 to 3
Outputs:
- grad_inputs: bfloat16 [1024, 12288], P('gx', 'gy')
- grad_w_first: bfloat16 [12288, 24576], P('gy', ('gx', 'gz'))
- grad_w_second: bfloat16 [24576, 12288], P(('gx', 'gz'), 'gy')
All inputs are finite; a program needn't handle non-finite values.
Results may differ from a plain program's by a relative error of at most 0.0049.
Values may be sent and summed in bfloat16 or wider, within the bound.
No kernel may reach another device: no remote copies, remote signals or barrier semaphores. Data moves between devices by JAX's collectives and lax.ppermute only.
A program may use at most 128 MiB of HBM per device.

v0:
```python
import math

import jax
import jax.numpy as jnp
from jax import lax
from jax.sharding import PartitionSpec as P

root_coef = math.sqrt(2.0 / math.pi)
cubic_coef = 0.044715


def gelu_local(pre, grad_hidden):
    inner = root_coef * (pre + cubic_coef * pre * pre * pre)
    tanh_val = jnp.tanh(inner)
    value = 0.5 * pre * (1.0 + tanh_val)
    slope = 0.5 * (1.0 + tanh_val) + 0.5 * pre * (1.0 - tanh_val * tanh_val) * root_coef * (
        1.0 + 3.0 * cubic_coef * pre * pre
    )
    return (value.astype(jnp.bfloat16), (grad_hidden * slope).astype(jnp.bfloat16))


def on_device(saved_inputs, w_first, w_second, grad_output):
    full_inputs, full_grads = (
        lax.all_gather(saved_inputs, "gx", axis=0, tiled=True),
        lax.all_gather(grad_output, "gx", axis=0, tiled=True),
    )
    pre_part = jnp.dot(full_inputs, w_first, preferred_element_type=jnp.float32)
    grad_part = lax.dot_general(
        full_grads, w_second, (((1,), (1,)), ((), ())), preferred_element_type=jnp.float32
    )
    pre_total, grad_total = lax.psum((pre_part, grad_part), "gy")
    hidden, grad_pre = gelu_local(pre_total, grad_total)
    grad_w_second = lax.dot_general(
        hidden, full_grads, (((0,), (0,)), ((), ())), preferred_element_type=jnp.float32
    ).astype(jnp.bfloat16)
    grad_w_first = lax.dot_general(
        full_inputs, grad_pre, (((0,), (0,)), ((), ())), preferred_element_type=jnp.float32
    ).astype(jnp.bfloat16)
    group_part = lax.psum_scatter(
        lax.dot_general(
            grad_pre, w_first, (((1,), (1,)), ((), ())), preferred_element_type=jnp.float32
        ),
        "gx",
        scatter_dimension=0,
        tiled=True,
    )
    grad_inputs = lax.psum(group_part, "gz").astype(jnp.bfloat16)
    return (grad_inputs, grad_w_first, grad_w_second)


def solution(mesh):
    in_specs = (P("gx", "gy"), P("gy", ("gx", "gz")), P(("gx", "gz"), "gy"), P("gx", "gy"))
    out_specs = (P("gx", "gy"), P("gy", ("gx", "gz")), P(("gx", "gz"), "gy"))
    return jax.shard_map(
        on_device, mesh=mesh, in_specs=in_specs, out_specs=out_specs, check_vma=False
    )
```

profile of v0, /device:TPU:2, one launch (start us, length us, event | category | flops | bytes accessed | tf_op | source)
XLA Modules:
  0.0 374.1 jit_solution(14548514815140006428)
XLA Ops:
  7.2 0.0 copy-start
  7.2 0.0 all-gather.3.cloned.1.call-start
  7.2 0.7 all-gather.3.cloned.1.call-update
  7.9 0.0 all-gather.5.cloned.1.call-start
  8.0 0.7 all-gather.5.cloned.1.call-update
  8.7 0.0 all-reduce.4.cloned.1.call-start
  8.7 49.1 %all-gather.3.cloned.1.call-done = bf16[1024,1536]{1,0:T(8,128)(2,1)} async-done(((bf16[128,1536]{1,0:T(8,128)(2,1)}), bf16[1024,1536]{1,0:T(8,128)(2,1)}) %all-gather.3.cloned.1.call-update) | async-done | bytes 3145744 | tf_op jit(solution)/shard_map/all_gather | solution.py:25
  57.8 6.9 %fusion.16 = f32[1024,768]{1,0:T(8,128)} fusion(bf16[1024,1536]{1,0:T(8,128)(2,1)} %all-gather.3.cloned.1.call-done, bf16[768,1536]{1,0:T(8,128)(2,1)} %param.6), kind=kOutput, calls=%fused_computation.21 | convolution fusion | flops 2415919104 | bytes 8650752 | tf_op jit(solution)/shard_map/dot_general | solution.py:28
  64.7 38.5 %all-gather.5.cloned.1.call-done = bf16[1024,1536]{1,0:T(8,128)(2,1)} async-done(((bf16[128,1536]{1,0:T(8,128)(2,1)}), bf16[1024,1536]{1,0:T(8,128)(2,1)}) %all-gather.5.cloned.1.call-update) | async-done | bytes 3145744 | tf_op jit(solution)/shard_map/all_gather | solution.py:24
  103.2 0.0 copy-done
  103.2 6.1 %fusion.17 = f32[1024,768]{1,0:T(8,128)} fusion(bf16[1024,1536]{1,0:T(8,128)(2,1)} %all-gather.5.cloned.1.call-done, bf16[1536,768]{1,0:T(8,128)(2,1)S(1)} %copy-done), kind=kOutput, calls=%fused_computation.22 | convolution fusion | flops 2415919104 | bytes 8650752 | tf_op jit(solution)/shard_map/dot_general | solution.py:27
  109.4 0.0 all-reduce.4.cloned.1.call-update
  109.4 0.0 reduce-scatter.2.cloned.1.call-start
  109.4 147.0 %all-reduce.4.cloned.1.call-done = (f32[1024,768]{1,0:T(8,128)}, f32[1024,768]{1,0:T(8,128)}) async-done(((f32[1024,768]{1,0:T(8,128)}, f32[1024,768]{1,0:T(8,128)}), (f32[1024,768]{1,0:T(8,128)}, f32[1024,768]{1,0:T(8,128)})) %all-reduce.4.cloned.1.call-update) | async-done | bytes 6291472 | tf_op jit(solution)/shard_map/psum | solution.py:31
  256.4 3.9 %fusion.6 = bf16[1024,768]{1,0:T(8,128)(2,1)S(1)} fusion(f32[1024,768]{1,0:T(8,128)} %get-tuple-element.6, f32[1024,768]{1,0:T(8,128)} %get-tuple-element.7), kind=kLoop, calls=%fused_computation.10 | loop fusion | flops 14942208 | bytes 7864320 | tf_op jit(solution)/shard_map/convert_element_type | solution.py:19
  260.3 0.0 copy-start.1
  260.3 1.1 copy-done.1
  261.4 4.7 %fusion.18 = f32[1024,1536]{1,0:T(8,128)} fusion(bf16[1024,768]{1,0:T(8,128)(2,1)S(1)} %fusion.6, bf16[1536,768]{1,0:T(8,128)(2,1)S(1)} %copy-done), kind=kOutput, calls=%fused_computation.23 | convolution fusion | flops 2415919104 | bytes 10223616 | tf_op jit(solution)/shard_map/dot_general | solution.py:40
  266.1 0.0 reduce-scatter.2.cloned.1.call-update
  266.1 6.4 %fusion.7 = bf16[1536,768]{0,1:T(8,128)(2,1)} fusion(bf16[1024,768]{1,0:T(8,128)(2,1)} %copy-done.1, bf16[1024,1536]{1,0:T(8,128)(2,1)} %all-gather.5.cloned.1.call-done), kind=kOutput, calls=%fused_computation.12 | convolution fusion | flops 2417098752 | bytes 7077888 | tf_op jit(solution)/shard_map/dot_general | solution.py:36
  272.5 4.3 %copy.7 = bf16[1536,768]{1,0:T(8,128)(2,1)} copy(bf16[1536,768]{0,1:T(8,128)(2,1)} %fusion.7) | data formatting | bytes 4718592
  276.8 7.6 %convolution_convert_fusion = bf16[768,1536]{1,0:T(8,128)(2,1)} fusion(bf16[1024,1536]{1,0:T(8,128)(2,1)} %all-gather.3.cloned.1.call-done, f32[1024,768]{1,0:T(8,128)} %get-tuple-element.7), kind=kOutput, calls=%fused_computation.2 | convolution fusion | flops 2424176640 | bytes 8650752 | tf_op jit(solution)/shard_map/dot_general | solution.py:33
  284.4 58.0 %reduce-scatter.2.cloned.1.call-done = f32[128,1536]{1,0:T(8,128)} async-done(((f32[1024,1536]{1,0:T(8,128)}), f32[128,1536]{1,0:T(8,128)}) %reduce-scatter.2.cloned.1.call-update) | async-done | bytes 786448 | tf_op jit(solution)/shard_map/reduce_scatter | solution.py:39
  342.4 25.2 %all-reduce.5 = bf16[128,1536]{1,0:T(8,128)(2,1)} all-reduce(f32[128,1536]{1,0:T(8,128)} %reduce-scatter.2.cloned.1.call-done), channel_id=1, replica_groups=mesh['gx'=8,'gy'=8,'gz'=4] {'gz'}, use_global_device_ids=true, to_apply=%region_3.0 | all-reduce | flops 196608 | bytes 1179648 | tf_op jit(solution)/shard_map/psum | solution.py:47
Async XLA Ops:
  7.2 96.0 %copy-start = (bf16[1536,768]{1,0:T(8,128)(2,1)S(1)}, bf16[1536,768]{1,0:T(8,128)(2,1)}, u32[]{:S(2)}) copy-start(bf16[1536,768]{1,0:T(8,128)(2,1)} %param.5) | copy-start | bytes 7077892
  7.2 50.6 %all-gather.3.cloned.1.call-start = ((), (), s32[]{:S(2)}) async-start(), calls=%async_computation.1 | async-start | bytes 3538944 | tf_op jit(solution)/shard_map/all_gather | solution.py:25
  7.9 95.3 %all-gather.5.cloned.1.call-start = ((), (), s32[]{:S(2)}) async-start(), calls=%async_computation.2 | async-start | bytes 3538944 | tf_op jit(solution)/shard_map/all_gather | solution.py:24
  8.7 247.7 %all-reduce.4.cloned.1.call-start = ((), (), s32[]{:S(2)}) async-start(), calls=%async_computation.4 | async-start | bytes 12582912 | tf_op jit(solution)/shard_map/psum | solution.py:31
  109.4 233.0 %reduce-scatter.2.cloned.1.call-start = ((), (), s32[]{:S(2)}) async-start(), calls=%async_computation.3 | async-start | bytes 7077888 | tf_op jit(solution)/shard_map/reduce_scatter | solution.py:39
  260.3 1.1 copy-start.1
Sparse Core Ops, SparseCore 0:
  9.8 47.9 all-gather.2
  59.6 43.6 all-gather.4
  109.5 146.8 all-reduce.3
  266.2 76.0 reduce-scatter.1
where the time goes:
time: 374 us
  waiting for transfers between devices  294 us (79%)
  matrix products  31.8 us (9%)
  blocking collectives  25.2 us (7%)
  between operations  13.8 us (4%)
  local copies, waits for them, and re-layouts  5.41 us (1%)
  other arithmetic  3.9 us (1%)
    psum x1, waiting for transfers between devices, on_device(): pre_total, grad_total = lax.psum((pre_part, grad_part), 'gy')  147 us
    reduce_scatter x1, waiting for transfers between devices, on_device(): lax.psum_scatter(lax.dot_general(grad_pre, w_first, (((1,), (1,)), ((), (...  58 us
    all_gather x1, waiting for transfers between devices, on_device(): lax.all_gather(grad_output, 'gx', axis=0, tiled=True)  49.1 us
    all_gather x1, waiting for transfers between devices, on_device(): lax.all_gather(saved_inputs, 'gx', axis=0, tiled=True)  38.5 us
    psum x1, blocking collectives, on_device(): grad_inputs = lax.psum(group_part, 'gz').astype(jnp.bfloat16)  25.2 us
    dot_general x1, matrix products, on_device(): lax.dot_general(hidden, full_grads, (((0,), (0,)), ((), ())), preferred_e...  7.61 us
  transfers between devices with their start and end apart: 4, of which 4 were waited for; matrix products, arithmetic and copies ran while one was open for 7% of the time, Pallas kernels for 0%

commit v1 on v0

v1 whole, which is shorter than its diff:
```python
import math

import jax
import jax.numpy as jnp
from jax import lax
from jax.sharding import Mesh, PartitionSpec as P

root_coef = math.sqrt(2.0 / math.pi)
cubic_coef = 0.044715
BF = jnp.bfloat16
F32 = jnp.float32
GY = ("ylo", "x")
GROUPS = ((0, 1, -1), (2, -2), (3, -3, 4))


def gelu_local(pre, grad_hidden):
    inner = root_coef * (pre + cubic_coef * pre * pre * pre)
    tanh_val = jnp.tanh(inner)
    value = 0.5 * pre * (1.0 + tanh_val)
    slope = 0.5 * (1.0 + tanh_val) + 0.5 * pre * (1.0 - tanh_val * tanh_val) * root_coef * (
        1.0 + 3.0 * cubic_coef * pre * pre
    )
    return (value.astype(BF), (grad_hidden * slope).astype(BF))


def shift(a, axis, size, by):
    return lax.ppermute(a, axis, [(i, (i + by) % size) for i in range(size)])


def swap(a, axis):
    return lax.ppermute(a, axis, [(0, 1), (1, 0)])


def dot(a, b, ca, cb):
    return lax.dot_general(a, b, (((ca,), (cb,)), ((), ())), preferred_element_type=F32)


def on_device(x, w1, w2, g):
    nz = lax.axis_size("z")
    core = lax.axis_index("core")
    half = x.shape[0] // 2
    ff = w1.shape[1]
    ngy = lax.axis_size("ylo") * lax.axis_size("x")

    def part(a, which):
        return lax.dynamic_slice_in_dim(a, which * half, half, 0)

    pack = jnp.stack([part(x, core), part(g, core)])
    shards = {0: (part(x, core), part(g, core), part(x, 1 - core), part(g, 1 - core))}
    up = down = pack
    for k in range(1, nz // 2):
        up, down = shift(up, "z", nz, 1), shift(down, "z", nz, -1)
        for d, mine in ((k, up), (-k, down)):
            other = swap(mine, "core")
            shards[d] = (mine[0], mine[1], other[0], other[1])
    xs, gs = shift(up[0], "z", nz, 1), shift(down[1], "z", nz, -1)
    shards[nz // 2] = (xs, gs, swap(xs, "core"), swap(gs, "core"))

    chunks = []
    for group in GROUPS:
        xc = jnp.concatenate([shards[d][i] for d in group for i in (0, 2)])
        gc = jnp.concatenate([shards[d][i] for d in group for i in (1, 3)])
        rows = xc.shape[0] // ngy
        sums = jnp.concatenate([dot(xc, w1, 1, 0).astype(BF), dot(gc, w2, 1, 1).astype(BF)], axis=1)
        got = lax.all_to_all(sums.reshape(ngy, rows, 2 * ff), GY, 0, 0)
        total = jnp.sum(got.astype(F32), axis=0)
        hid, gp = gelu_local(total[:, :ff], total[:, ff:])
        act = jnp.concatenate([hid, gp], axis=1)
        acts = lax.all_to_all(jnp.broadcast_to(act[None], (ngy, rows, 2 * ff)), GY, 0, 0)
        acts = acts.reshape(ngy * rows, 2 * ff)
        chunks.append((group, xc, gc, acts[:, :ff], acts[:, ff:]))

    own = None
    for group, xc, gc, hid, gp in chunks:
        back = dot(gp, w1, 1, 1)
        for n, d in enumerate(group):
            mine = back[2 * n * half : (2 * n + 1) * half]
            other = back[(2 * n + 1) * half : (2 * n + 2) * half]
            both = mine + swap(other.astype(BF), "core").astype(F32)
            if d:
                both = shift(both.astype(BF), "z", nz, -d).astype(F32)
            own = both if own is None else own + both
    own = own + swap(own.astype(BF), "yhi").astype(F32)
    own = own.astype(BF)
    theirs = swap(own, "core")
    first = core == 0
    grad_inputs = jnp.concatenate([jnp.where(first, own, theirs), jnp.where(first, theirs, own)])

    x_all = jnp.concatenate([c[1] for c in chunks])
    g_all = jnp.concatenate([c[2] for c in chunks])
    hid_all = jnp.concatenate([c[3] for c in chunks])
    gp_all = jnp.concatenate([c[4] for c in chunks])
    grad_w_second = dot(hid_all, g_all, 0, 0).astype(BF)
    grad_w_first = dot(x_all, gp_all, 0, 0).astype(BF)
    return (grad_inputs, grad_w_first, grad_w_second)


def solution(mesh):
    devices = mesh.devices.reshape(mesh.devices.shape[0], 2, -1, 2, 2)
    fine = Mesh(devices, ("z", "ylo", "x", "yhi", "core"))
    units = ("z", "yhi", "core")
    in_specs = (P("z", GY), P(GY, units), P(units, GY), P("z", GY))
    out_specs = (P("z", GY), P(GY, units), P(units, GY))
    return jax.shard_map(
        on_device, mesh=fine, in_specs=in_specs, out_specs=out_specs, check_vma=False
    )
```

time: 374 us -> 238 us (0.64)
  waiting for transfers between devices: 294 us -> 83.4 us
  starting transfers between devices: 0.16 us -> 70.8 us
  local copies, waits for them, and re-layouts: 5.41 us -> 39.6 us
  blocking collectives: 25.2 us -> 0 us
  between operations: 13.8 us -> 1.04 us
  other arithmetic: 3.9 us -> 13.2 us
  matrix products: 31.8 us -> 27.1 us
    psum x1 -> x0, waiting for transfers between devices: 147 us -> none  [on_device(): pre_total, grad_total = lax.psum((pre_part, grad_part), 'gy')]
    all_gather x2 -> x0, waiting for transfers between devices: 87.6 us -> none  [the longest x1 49.1 us: on_device(): lax.all_gather(grad_output, 'gx', axis=0, tiled=True)]
    reduce_scatter x1 -> x0, waiting for transfers between devices: 58 us -> none  [on_device(): lax.psum_scatter(lax.dot_general(grad_pre, w_first, (((1,), (1,)), ((), (...]
    all_to_all x0 -> x6, waiting for transfers between devices: none -> 49.2 us  [the longest x3 26.8 us: on_device(): lax.all_to_all(jnp.broadcast_to(act[None], (ngy, rows, 2 * ff)), GY, 0, 0)]
    ppermute x0 -> x33, starting transfers between devices: none -> 40.1 us  [the longest x15 32.6 us: shift(): return lax.ppermute(a, axis, [(i, (i + by) % size) for i in range(size)])]
    ppermute x0 -> x33, waiting for transfers between devices: none -> 34.1 us  [the longest x15 34.1 us: shift(): return lax.ppermute(a, axis, [(i, (i + by) % size) for i in range(size)])]
    all_to_all x0 -> x6, starting transfers between devices: none -> 30.7 us  [the longest x3 16.9 us: on_device(): got = lax.all_to_all(sums.reshape(ngy, rows, 2 * ff), GY, 0, 0)]
    psum x1 -> x0, blocking collectives: 25.2 us -> none  [on_device(): grad_inputs = lax.psum(group_part, 'gz').astype(jnp.bfloat16)]
  transfers between devices with their start and end apart: 4 -> 39, of which waited for: 4 -> 10; matrix products, arithmetic and copies ran while one was open for 7% -> 29% of each run, Pallas kernels for 0% -> 0%
where the time goes in v1:
time: 238 us; the launch traced here: 235 us
  waiting for transfers between devices  83.4 us (35%)
  starting transfers between devices  70.8 us (30%)
  local copies, waits for them, and re-layouts  39.6 us (17%)
  matrix products  27.1 us (11%)
  other arithmetic  13.2 us (6%)
    ppermute x15, waiting for transfers between devices, shift(): return lax.ppermute(a, axis, [(i, (i + by) % size) for i in range(size)])  34.1 us
    ppermute x15, starting transfers between devices, shift(): return lax.ppermute(a, axis, [(i, (i + by) % size) for i in range(size)])  32.6 us
    dot_general x11, matrix products, dot(): lax.dot_general(a, b, (((ca,), (cb,)), ((), ())), preferred_element_type=...  27.1 us
    all_to_all x3, waiting for transfers between devices, on_device(): lax.all_to_all(jnp.broadcast_to(act[None], (ngy, rows, 2 * ff)), GY, 0, 0)  26.8 us
    unnamed x71, local copies, waits for them, and re-layouts  26.4 us
    all_to_all x3, waiting for transfers between devices, on_device(): got = lax.all_to_all(sums.reshape(ngy, rows, 2 * ff), GY, 0, 0)  22.4 us
    all_to_all x3, starting transfers between devices, on_device(): got = lax.all_to_all(sums.reshape(ngy, rows, 2 * ff), GY, 0, 0)  16.9 us
    all_to_all x3, starting transfers between devices, on_device(): lax.all_to_all(jnp.broadcast_to(act[None], (ngy, rows, 2 * ff)), GY, 0, 0)  13.9 us
  transfers between devices with their start and end apart: 39, of which 10 were waited for; matrix products, arithmetic and copies ran while one was open for 29% of the time, Pallas kernels for 0%

profile of v1, /device:TPU:2, one launch (start us, length us, event | category | flops | bytes accessed | tf_op | source)
XLA Modules:
  0.0 235.1 jit_solution(1980726339916994775)
XLA Ops:
  4.1 2.1 dynamic-slice_dynamic-update-slice_fusion
  8.2 4.0 %collective-permute-start.2 = (bf16[2,64,1536]{2,1,0:T(8,128)(2,1)S(1)}, bf16[2,64,1536]{2,1,0:T(8,128)(2,1)}, u32[]{:S(2)}, u32[]{:S(2)}) collective-permute-start(bf16[2,64,1536]{2,1,0:T(8,128)(2,1)S(1)} %pad_maximum_fusion.3), channel_id=1, source_target_pairs={{0,224},{32,0},{64,32},{96,64},{128,96},{160,128},{192,160},{224,1... | collective-permute-start | bytes 1179656 | tf_op jit(solution)/shard_map/ppermute | solution.py:27
  13.7 7.7 %collective-permute-done = bf16[2,64,1536]{2,1,0:T(8,128)(2,1)} collective-permute-done((bf16[2,64,1536]{2,1,0:T(8,128)(2,1)S(1)}, bf16[2,64,1536]{2,1,0:T(8,128)(2,1)}, u32[]{:S(2)}, u32[]{:S(2)}) %collective-permute-start) | collective-permute-done | bytes 393248 | tf_op jit(solution)/shard_map/ppermute | solution.py:27
  21.9 3.0 %collective-permute-start.11 = (bf16[2,64,1536]{2,1,0:T(8,128)(2,1)}, bf16[2,64,1536]{2,1,0:T(8,128)(2,1)S(1)}, u32[]{:S(2)}, u32[]{:S(2)}) collective-permute-start(bf16[2,64,1536]{2,1,0:T(8,128)(2,1)} %collective-permute-done.2), channel_id=1, source_target_pairs={{0,224},{32,0},{64,32},{96,64},{128,96},{160,128},{192,160},{224,1... | collective-permute-start | bytes 1179656 | tf_op jit(solution)/shard_map/ppermute | solution.py:27
  30.7 2.5 %convolution_convert_fusion.4 = bf16[384,768]{1,0:T(8,128)(2,1)S(1)} fusion(bf16[384,1536]{1,0:T(8,128)(2,1)} %get-tuple-element.52, bf16[768,1536]{1,0:T(8,128)(2,1)S(1)} %copy-done.24), kind=kOutput, calls=%fused_computation.17 | convolution fusion | flops 906264576 | bytes 4128768 | tf_op jit(solution)/shard_map/dot_general | solution.py:35
  36.0 3.0 %collective-permute-start.19 = (bf16[2,64,1536]{2,1,0:T(8,128)(2,1)S(1)}, bf16[2,64,1536]{2,1,0:T(8,128)(2,1)S(1)}, u32[]{:S(2)}, u32[]{:S(2)}) collective-permute-start(bf16[2,64,1536]{2,1,0:T(8,128)(2,1)S(1)} %collective-permute-done.11), channel_id=1, source_target_pairs={{0,224},{32,0},{64,32},{96,64},{128,96},{160,128},{192,160},{224,1... | collective-permute-start | bytes 1179656 | tf_op jit(solution)/shard_map/ppermute | solution.py:27
  39.8 8.1 %collective-permute-done.19 = bf16[2,64,1536]{2,1,0:T(8,128)(2,1)S(1)} collective-permute-done((bf16[2,64,1536]{2,1,0:T(8,128)(2,1)S(1)}, bf16[2,64,1536]{2,1,0:T(8,128)(2,1)S(1)}, u32[]{:S(2)}, u32[]{:S(2)}) %collective-permute-start.19) | collective-permute-done | bytes 393248 | tf_op jit(solution)/shard_map/ppermute | solution.py:27
  48.6 3.7 %collective-permute-start.23 = (bf16[64,1536]{1,0:T(8,128)(2,1)}, bf16[64,1536]{1,0:T(8,128)(2,1)}, u32[]{:S(2)}, u32[]{:S(2)}) collective-permute-start(bf16[64,1536]{1,0:T(8,128)(2,1)} %slice_bitcast_fusion.1), channel_id=1, source_target_pairs={{0,224},{32,0},{64,32},{96,64},{128,96},{160,128},{192,160},{224,1... | collective-permute-start | bytes 589832 | tf_op jit(solution)/shard_map/ppermute | solution.py:27
  56.5 5.8 %all-to-all-start.2 = ((bf16[8,32,1536]{2,1,0:T(8,128)(2,1)}), bf16[8,32,1536]{2,1,0:T(8,128)(2,1)S(1)}, u32[]{:S(2)}, u32[]{:S(2)}) async-start(bf16[8,32,1536]{2,1,0:T(8,128)(2,1)} %bitcast.20), calls=%async_computation.2 | async-start | bytes 1572864 | tf_op jit(solution)/shard_map/all_to_all | solution.py:65
  78.2 5.7 %all-to-all-start = ((bf16[8,48,1536]{2,1,0:T(8,128)(2,1)}), bf16[8,48,1536]{2,1,0:T(8,128)(2,1)S(1)}, u32[]{:S(2)}, u32[]{:S(2)}) async-start(bf16[8,48,1536]{2,1,0:T(8,128)(2,1)} %bitcast.10), calls=%async_computation | async-start | bytes 2359296 | tf_op jit(solution)/shard_map/all_to_all | solution.py:65
  85.6 3.2 %convolution_convert_fusion.3 = bf16[384,768]{1,0:T(8,128)(2,1)} fusion(bf16[384,1536]{1,0:T(8,128)(2,1)} %get-tuple-element.91, bf16[1536,768]{1,0:T(8,128)(2,1)S(1)} %copy-done), kind=kOutput, calls=%fused_computation.16 | convolution fusion | flops 906264576 | bytes 4128768 | tf_op jit(solution)/shard_map/dot_general | solution.py:35
  89.7 10.4 %all-to-all-done = bf16[8,48,1536]{2,1,0:T(8,128)(2,1)S(1)} async-done(((bf16[8,48,1536]{2,1,0:T(8,128)(2,1)}), bf16[8,48,1536]{2,1,0:T(8,128)(2,1)S(1)}, u32[]{:S(2)}, u32[]{:S(2)}) %all-to-all-start) | async-done | bytes 1179680 | tf_op jit(solution)/shard_map/all_to_all | solution.py:65
  102.1 4.6 %all-to-all-start.3 = ((bf16[8,32,1536]{2,1,0:T(8,128)(2,1)}), bf16[8,32,1536]{2,1,0:T(8,128)(2,1)S(1)}, u32[]{:S(2)}, u32[]{:S(2)}) async-start(bf16[8,32,1536]{2,1,0:T(8,128)(2,1)} %broadcast_in_dim.7), calls=%async_computation.3 | async-start | bytes 1572864 | tf_op jit(solution)/shard_map/all_to_all | solution.py:69
  106.7 2.4 %pad_maximum_fusion.1 = bf16[384,1536]{1,0:T(8,128)(2,1)} fusion(bf16[384,768]{1,0:T(8,128)(2,1)} %convolution_convert_fusion.2, bf16[384,768]{1,0:T(8,128)(2,1)} %convolution_convert_fusion.3), kind=kLoop, calls=%fused_computation.22 | loop fusion | flops 2359296 | bytes 2359296 | tf_op jit(solution)/shard_map/concatenate | solution.py:64
  109.5 9.2 %all-to-all-done.3 = bf16[8,32,1536]{2,1,0:T(8,128)(2,1)S(1)} async-done(((bf16[8,32,1536]{2,1,0:T(8,128)(2,1)}), bf16[8,32,1536]{2,1,0:T(8,128)(2,1)S(1)}, u32[]{:S(2)}, u32[]{:S(2)}) %all-to-all-start.3) | async-done | bytes 786464 | tf_op jit(solution)/shard_map/all_to_all | solution.py:69
  118.6 5.3 %all-to-all-start.4 = ((bf16[8,48,1536]{2,1,0:T(8,128)(2,1)}), bf16[8,48,1536]{2,1,0:T(8,128)(2,1)}, u32[]{:S(2)}, u32[]{:S(2)}) async-start(bf16[8,48,1536]{2,1,0:T(8,128)(2,1)} %bitcast.159), calls=%async_computation.4 | async-start | bytes 2359296 | tf_op jit(solution)/shard_map/all_to_all | solution.py:65
  128.1 12.0 %all-to-all-done.4 = bf16[8,48,1536]{2,1,0:T(8,128)(2,1)} async-done(((bf16[8,48,1536]{2,1,0:T(8,128)(2,1)}), bf16[8,48,1536]{2,1,0:T(8,128)(2,1)}, u32[]{:S(2)}, u32[]{:S(2)}) %all-to-all-start.4) | async-done | bytes 1179680 | tf_op jit(solution)/shard_map/all_to_all | solution.py:65
  141.3 4.6 %all-to-all-start.1 = ((bf16[8,48,1536]{2,1,0:T(8,128)(2,1)}), bf16[8,48,1536]{2,1,0:T(8,128)(2,1)S(1)}, u32[]{:S(2)}, u32[]{:S(2)}) async-start(bf16[8,48,1536]{2,1,0:T(8,128)(2,1)} %broadcast_in_dim.6), calls=%async_computation.1 | async-start | bytes 2359296 | tf_op jit(solution)/shard_map/all_to_all | solution.py:69
  150.1 2.2 collective-permute-start.16
  154.2 7.8 %all-to-all-done.1 = bf16[8,48,1536]{2,1,0:T(8,128)(2,1)S(1)} async-done(((bf16[8,48,1536]{2,1,0:T(8,128)(2,1)}), bf16[8,48,1536]{2,1,0:T(8,128)(2,1)S(1)}, u32[]{:S(2)}, u32[]{:S(2)}) %all-to-all-start.1) | async-done | bytes 1179680 | tf_op jit(solution)/shard_map/all_to_all | solution.py:69
  162.0 2.2 broadcast_in_dim.8
  164.2 4.6 %all-to-all-start.5 = ((bf16[8,48,1536]{2,1,0:T(8,128)(2,1)}), bf16[8,48,1536]{2,1,0:T(8,128)(2,1)S(1)}, u32[]{:S(2)}, u32[]{:S(2)}) async-start(bf16[8,48,1536]{2,1,0:T(8,128)(2,1)} %broadcast_in_dim.8), calls=%async_computation.5 | async-start | bytes 2359296 | tf_op jit(solution)/shard_map/all_to_all | solution.py:69
  168.8 3.7 %fusion.107 = (bf16[384,1536]{1,0:T(8,128)(2,1)S(1)}, f32[384,1536]{1,0:T(8,128)}) fusion(bf16[1536,768]{1,0:T(8,128)(2,1)S(1)} %copy-done, bf16[384,1536]{1,0:T(8,128)(2,1)} %bitcast.155), kind=kOutput, calls=%fused_computation.199 | convolution fusion | flops 906559488 | bytes 6488064 | tf_op jit(solution)/shard_map/dot_general | solution.py:35
  175.1 9.9 %all-to-all-done.5 = bf16[8,48,1536]{2,1,0:T(8,128)(2,1)S(1)} async-done(((bf16[8,48,1536]{2,1,0:T(8,128)(2,1)}), bf16[8,48,1536]{2,1,0:T(8,128)(2,1)S(1)}, u32[]{:S(2)}, u32[]{:S(2)}) %all-to-all-start.5) | async-done | bytes 1179680 | tf_op jit(solution)/shard_map/all_to_all | solution.py:69
  188.7 3.4 %collective-permute-start.6 = (bf16[64,1536]{1,0:T(8,128)(2,1)S(1)}, bf16[64,1536]{1,0:T(8,128)(2,1)S(1)}, u32[]{:S(2)}, u32[]{:S(2)}) collective-permute-start(bf16[64,1536]{1,0:T(8,128)(2,1)S(1)} %get-tuple-element.5), channel_id=1, source_target_pairs={{0,224},{32,0},{64,32},{96,64},{128,96},{160,128},{192,160},{224,1... | collective-permute-start | bytes 589832 | tf_op jit(solution)/shard_map/ppermute | solution.py:27
  192.2 4.3 %collective-permute-start.30 = (bf16[64,1536]{1,0:T(8,128)(2,1)S(1)}, bf16[64,1536]{1,0:T(8,128)(2,1)S(1)}, u32[]{:S(2)}, u32[]{:S(2)}) collective-permute-start(bf16[64,1536]{1,0:T(8,128)(2,1)S(1)} %get-tuple-element.8), channel_id=1, source_target_pairs={{0,128},{32,160},{64,192},{96,224},{128,0},{160,32},{192,64},{224,... | collective-permute-start | bytes 589832 | tf_op jit(solution)/shard_map/ppermute | solution.py:27
  197.5 4.0 %collective-permute-start.26 = (bf16[64,1536]{1,0:T(8,128)(2,1)S(1)}, bf16[64,1536]{1,0:T(8,128)(2,1)S(1)}, u32[]{:S(2)}, u32[]{:S(2)}) collective-permute-start(bf16[64,1536]{1,0:T(8,128)(2,1)S(1)} %get-tuple-element.7), channel_id=1, source_target_pairs={{0,160},{32,192},{64,224},{96,0},{128,32},{160,64},{192,96},{224,1... | collective-permute-start | bytes 589832 | tf_op jit(solution)/shard_map/ppermute | solution.py:27
  201.6 9.4 %collective-permute-done.6 = bf16[64,1536]{1,0:T(8,128)(2,1)S(1)} collective-permute-done((bf16[64,1536]{1,0:T(8,128)(2,1)S(1)}, bf16[64,1536]{1,0:T(8,128)(2,1)S(1)}, u32[]{:S(2)}, u32[]{:S(2)}) %collective-permute-start.6) | collective-permute-done | bytes 196640 | tf_op jit(solution)/shard_map/ppermute | solution.py:27
  211.1 8.7 %collective-permute-done.28 = bf16[64,1536]{1,0:T(8,128)(2,1)S(1)} collective-permute-done((bf16[64,1536]{1,0:T(8,128)(2,1)S(1)}, bf16[64,1536]{1,0:T(8,128)(2,1)S(1)}, u32[]{:S(2)}, u32[]{:S(2)}) %collective-permute-start.28) | collective-permute-done | bytes 196640 | tf_op jit(solution)/shard_map/ppermute | solution.py:27
  221.0 3.0 %collective-permute-start.31 = (bf16[64,1536]{1,0:T(8,128)(2,1)S(1)}, bf16[64,1536]{1,0:T(8,128)(2,1)S(1)}, u32[]{:S(2)}, u32[]{:S(2)}) collective-permute-start(bf16[64,1536]{1,0:T(8,128)(2,1)S(1)} %get-tuple-element.3), channel_id=1, source_target_pairs={{0,2},{2,0},{1,3},{3,1},{4,6},{6,4},{5,7},{7,5},{8,10},{10,8},{9,1... | collective-permute-start | bytes 589832 | tf_op jit(solution)/shard_map/ppermute | solution.py:31
  224.1 6.1 %convolution_convert_fusion.1 = bf16[1536,768]{1,0:T(8,128)(2,1)} fusion(bf16[1024,1536]{1,0:T(8,128)(2,1)} %get-tuple-element.90, bf16[384,768]{1,0:T(8,128)(2,1)S(1)} %get-tuple-element.15, bf16[256,768]{1,0:T(8,128)(2,1)S(1)} %copy-done.20, bf16[384,768]{1,0:T(8,128)(2,1)S(1)} %copy-done.18), kind=kOutput, calls=%fused_computation.1 | convolution fusion | flops 2421817344 | bytes 7077888 | tf_op jit(solution)/shard_map/dot_general | solution.py:35
  230.4 3.9 %convolution_convert_fusion = bf16[768,1536]{1,0:T(8,128)(2,1)} fusion(bf16[1024,1536]{1,0:T(8,128)(2,1)S(1)} %copy-done.23, bf16[384,768]{1,0:T(8,128)(2,1)S(1)} %get-tuple-element.14, bf16[256,768]{1,0:T(8,128)(2,1)S(1)} %copy-done.19, bf16[384,768]{1,0:T(8,128)(2,1)S(1)} %copy-done.17), kind=kOutput, calls=%fused_computation | convolution fusion | flops 2421817344 | bytes 7077888 | tf_op jit(solution)/shard_map/dot_general | solution.py:35
  (165 shorter events, 63.4 us)
Async XLA Ops:
  6.2 15.2 %collective-permute-start = (bf16[2,64,1536]{2,1,0:T(8,128)(2,1)S(1)}, bf16[2,64,1536]{2,1,0:T(8,128)(2,1)}, u32[]{:S(2)}, u32[]{:S(2)}) collective-permute-start(bf16[2,64,1536]{2,1,0:T(8,128)(2,1)S(1)} %pad_maximum_fusion.3), channel_id=1, source_target_pairs={{0,32},{32,64},{64,96},{96,128},{128,160},{160,192},{192,224},{224... | collective-permute-start | bytes 1179656 | tf_op jit(solution)/shard_map/ppermute | solution.py:27
  8.2 13.2 %collective-permute-start.2 = (bf16[2,64,1536]{2,1,0:T(8,128)(2,1)S(1)}, bf16[2,64,1536]{2,1,0:T(8,128)(2,1)}, u32[]{:S(2)}, u32[]{:S(2)}) collective-permute-start(bf16[2,64,1536]{2,1,0:T(8,128)(2,1)S(1)} %pad_maximum_fusion.3), channel_id=1, source_target_pairs={{0,224},{32,0},{64,32},{96,64},{128,96},{160,128},{192,160},{224,1... | collective-permute-start | bytes 1179656 | tf_op jit(solution)/shard_map/ppermute | solution.py:27
  21.4 12.9 %collective-permute-start.9 = (bf16[2,64,1536]{2,1,0:T(8,128)(2,1)}, bf16[2,64,1536]{2,1,0:T(8,128)(2,1)S(1)}, u32[]{:S(2)}, u32[]{:S(2)}) collective-permute-start(bf16[2,64,1536]{2,1,0:T(8,128)(2,1)} %collective-permute-done), channel_id=1, source_target_pairs={{0,32},{32,64},{64,96},{96,128},{128,160},{160,192},{192,224},{224... | collective-permute-start | bytes 1179656 | tf_op jit(solution)/shard_map/ppermute | solution.py:27
  21.4 8.4 %collective-permute-start.3 = (bf16[2,64,1536]{2,1,0:T(8,128)(2,1)}, bf16[2,64,1536]{2,1,0:T(8,128)(2,1)S(1)}, u32[]{:S(2)}, u32[]{:S(2)}) collective-permute-start(bf16[2,64,1536]{2,1,0:T(8,128)(2,1)} %collective-permute-done.2), channel_id=1, source_target_pairs={{0,1},{1,0},{2,3},{3,2},{4,5},{5,4},{6,7},{7,6},{8,9},{9,8},{10,11... | collective-permute-start | bytes 1179656 | tf_op jit(solution)/shard_map/ppermute | solution.py:31
  21.9 13.6 %collective-permute-start.11 = (bf16[2,64,1536]{2,1,0:T(8,128)(2,1)}, bf16[2,64,1536]{2,1,0:T(8,128)(2,1)S(1)}, u32[]{:S(2)}, u32[]{:S(2)}) collective-permute-start(bf16[2,64,1536]{2,1,0:T(8,128)(2,1)} %collective-permute-done.2), channel_id=1, source_target_pairs={{0,224},{32,0},{64,32},{96,64},{128,96},{160,128},{192,160},{224,1... | collective-permute-start | bytes 1179656 | tf_op jit(solution)/shard_map/ppermute | solution.py:27
  34.3 18.7 %collective-permute-start.10 = (bf16[2,64,1536]{2,1,0:T(8,128)(2,1)S(1)}, bf16[2,64,1536]{2,1,0:T(8,128)(2,1)S(1)}, u32[]{:S(2)}, u32[]{:S(2)}) collective-permute-start(bf16[2,64,1536]{2,1,0:T(8,128)(2,1)S(1)} %collective-permute-done.9), channel_id=1, source_target_pairs={{0,1},{1,0},{2,3},{3,2},{4,5},{5,4},{6,7},{7,6},{8,9},{9,8},{10,11... | collective-permute-start | bytes 1179656 | tf_op jit(solution)/shard_map/ppermute | solution.py:31
  34.4 17.9 %collective-permute-start.17 = (bf16[2,64,1536]{2,1,0:T(8,128)(2,1)S(1)}, bf16[2,64,1536]{2,1,0:T(8,128)(2,1)S(1)}, u32[]{:S(2)}, u32[]{:S(2)}) collective-permute-start(bf16[2,64,1536]{2,1,0:T(8,128)(2,1)S(1)} %collective-permute-done.9), channel_id=1, source_target_pairs={{0,32},{32,64},{64,96},{96,128},{128,160},{160,192},{192,224},{224... | collective-permute-start | bytes 1179656 | tf_op jit(solution)/shard_map/ppermute | solution.py:27
  35.5 17.5 %collective-permute-start.12 = (bf16[2,64,1536]{2,1,0:T(8,128)(2,1)S(1)}, bf16[2,64,1536]{2,1,0:T(8,128)(2,1)S(1)}, u32[]{:S(2)}, u32[]{:S(2)}) collective-permute-start(bf16[2,64,1536]{2,1,0:T(8,128)(2,1)S(1)} %collective-permute-done.11), channel_id=1, source_target_pairs={{0,1},{1,0},{2,3},{3,2},{4,5},{5,4},{6,7},{7,6},{8,9},{9,8},{10,11... | collective-permute-start | bytes 1179656 | tf_op jit(solution)/shard_map/ppermute | solution.py:31
  36.0 11.9 %collective-permute-start.19 = (bf16[2,64,1536]{2,1,0:T(8,128)(2,1)S(1)}, bf16[2,64,1536]{2,1,0:T(8,128)(2,1)S(1)}, u32[]{:S(2)}, u32[]{:S(2)}) collective-permute-start(bf16[2,64,1536]{2,1,0:T(8,128)(2,1)S(1)} %collective-permute-done.11), channel_id=1, source_target_pairs={{0,224},{32,0},{64,32},{96,64},{128,96},{160,128},{192,160},{224,1... | collective-permute-start | bytes 1179656 | tf_op jit(solution)/shard_map/ppermute | solution.py:27
  48.6 19.6 %collective-permute-start.23 = (bf16[64,1536]{1,0:T(8,128)(2,1)}, bf16[64,1536]{1,0:T(8,128)(2,1)}, u32[]{:S(2)}, u32[]{:S(2)}) collective-permute-start(bf16[64,1536]{1,0:T(8,128)(2,1)} %slice_bitcast_fusion.1), channel_id=1, source_target_pairs={{0,224},{32,0},{64,32},{96,64},{128,96},{160,128},{192,160},{224,1... | collective-permute-start | bytes 589832 | tf_op jit(solution)/shard_map/ppermute | solution.py:27
  53.0 15.3 %collective-permute-start.21 = (bf16[64,1536]{1,0:T(8,128)(2,1)}, bf16[64,1536]{1,0:T(8,128)(2,1)}, u32[]{:S(2)}, u32[]{:S(2)}) collective-permute-start(bf16[64,1536]{1,0:T(8,128)(2,1)} %slice_bitcast_fusion.7), channel_id=1, source_target_pairs={{0,32},{32,64},{64,96},{96,128},{128,160},{160,192},{192,224},{224... | collective-permute-start | bytes 589832 | tf_op jit(solution)/shard_map/ppermute | solution.py:27
  56.5 20.7 %all-to-all-start.2 = ((bf16[8,32,1536]{2,1,0:T(8,128)(2,1)}), bf16[8,32,1536]{2,1,0:T(8,128)(2,1)S(1)}, u32[]{:S(2)}, u32[]{:S(2)}) async-start(bf16[8,32,1536]{2,1,0:T(8,128)(2,1)} %bitcast.20), calls=%async_computation.2 | async-start | bytes 1572864 | tf_op jit(solution)/shard_map/all_to_all | solution.py:65
  62.4 8.0 %collective-permute-start.20 = (bf16[2,64,1536]{2,1,0:T(8,128)(2,1)}, bf16[2,64,1536]{2,1,0:T(8,128)(2,1)S(1)}, u32[]{:S(2)}, u32[]{:S(2)}) collective-permute-start(bf16[2,64,1536]{2,1,0:T(8,128)(2,1)} %copy-done.13), channel_id=1, source_target_pairs={{0,1},{1,0},{2,3},{3,2},{4,5},{5,4},{6,7},{7,6},{8,9},{9,8},{10,11... | collective-permute-start | bytes 1179656 | tf_op jit(solution)/shard_map/ppermute | solution.py:31
  68.3 15.7 %collective-permute-start.22 = (bf16[64,1536]{1,0:T(8,128)(2,1)}, bf16[64,1536]{1,0:T(8,128)(2,1)}, u32[]{:S(2)}, u32[]{:S(2)}) collective-permute-start(bf16[64,1536]{1,0:T(8,128)(2,1)} %collective-permute-done.21), channel_id=1, source_target_pairs={{0,1},{1,0},{2,3},{3,2},{4,5},{5,4},{6,7},{7,6},{8,9},{9,8},{10,11... | collective-permute-start | bytes 589832 | tf_op jit(solution)/shard_map/ppermute | solution.py:31
  78.2 21.9 %all-to-all-start = ((bf16[8,48,1536]{2,1,0:T(8,128)(2,1)}), bf16[8,48,1536]{2,1,0:T(8,128)(2,1)S(1)}, u32[]{:S(2)}, u32[]{:S(2)}) async-start(bf16[8,48,1536]{2,1,0:T(8,128)(2,1)} %bitcast.10), calls=%async_computation | async-start | bytes 2359296 | tf_op jit(solution)/shard_map/all_to_all | solution.py:65
  102.1 16.5 %all-to-all-start.3 = ((bf16[8,32,1536]{2,1,0:T(8,128)(2,1)}), bf16[8,32,1536]{2,1,0:T(8,128)(2,1)S(1)}, u32[]{:S(2)}, u32[]{:S(2)}) async-start(bf16[8,32,1536]{2,1,0:T(8,128)(2,1)} %broadcast_in_dim.7), calls=%async_computation.3 | async-start | bytes 1572864 | tf_op jit(solution)/shard_map/all_to_all | solution.py:69
  118.6 21.5 %all-to-all-start.4 = ((bf16[8,48,1536]{2,1,0:T(8,128)(2,1)}), bf16[8,48,1536]{2,1,0:T(8,128)(2,1)}, u32[]{:S(2)}, u32[]{:S(2)}) async-start(bf16[8,48,1536]{2,1,0:T(8,128)(2,1)} %bitcast.159), calls=%async_computation.4 | async-start | bytes 2359296 | tf_op jit(solution)/shard_map/all_to_all | solution.py:65
  126.7 21.6 %collective-permute-start.13 = (bf16[64,1536]{1,0:T(8,128)(2,1)}, bf16[64,1536]{1,0:T(8,128)(2,1)}, u32[]{:S(2)}, u32[]{:S(2)}) collective-permute-start(bf16[64,1536]{1,0:T(8,128)(2,1)} %get-tuple-element.24), channel_id=1, source_target_pairs={{0,1},{1,0},{2,3},{3,2},{4,5},{5,4},{6,7},{7,6},{8,9},{9,8},{10,11... | collective-permute-start | bytes 589832 | tf_op jit(solution)/shard_map/ppermute | solution.py:31
  126.7 21.6 %collective-permute-start.15 = (bf16[64,1536]{1,0:T(8,128)(2,1)}, bf16[64,1536]{1,0:T(8,128)(2,1)}, u32[]{:S(2)}, u32[]{:S(2)}) collective-permute-start(bf16[64,1536]{1,0:T(8,128)(2,1)} %get-tuple-element.25), channel_id=1, source_target_pairs={{0,1},{1,0},{2,3},{3,2},{4,5},{5,4},{6,7},{7,6},{8,9},{9,8},{10,11... | collective-permute-start | bytes 589832 | tf_op jit(solution)/shard_map/ppermute | solution.py:31
  141.3 20.7 %all-to-all-start.1 = ((bf16[8,48,1536]{2,1,0:T(8,128)(2,1)}), bf16[8,48,1536]{2,1,0:T(8,128)(2,1)S(1)}, u32[]{:S(2)}, u32[]{:S(2)}) async-start(bf16[8,48,1536]{2,1,0:T(8,128)(2,1)} %broadcast_in_dim.6), calls=%async_computation.1 | async-start | bytes 2359296 | tf_op jit(solution)/shard_map/all_to_all | solution.py:69
  150.1 42.1 %collective-permute-start.16 = (bf16[64,1536]{1,0:T(8,128)(2,1)}, bf16[64,1536]{1,0:T(8,128)(2,1)}, u32[]{:S(2)}, u32[]{:S(2)}) collective-permute-start(bf16[64,1536]{1,0:T(8,128)(2,1)} %get-tuple-element.11), channel_id=1, source_target_pairs={{0,64},{32,96},{64,128},{96,160},{128,192},{160,224},{192,0},{224,... | collective-permute-start | bytes 589832 | tf_op jit(solution)/shard_map/ppermute | solution.py:27
  152.3 44.2 %collective-permute-start.14 = (bf16[64,1536]{1,0:T(8,128)(2,1)}, bf16[64,1536]{1,0:T(8,128)(2,1)}, u32[]{:S(2)}, u32[]{:S(2)}) collective-permute-start(bf16[64,1536]{1,0:T(8,128)(2,1)} %get-tuple-element.10), channel_id=1, source_target_pairs={{0,192},{32,224},{64,0},{96,32},{128,64},{160,96},{192,128},{224,1... | collective-permute-start | bytes 589832 | tf_op jit(solution)/shard_map/ppermute | solution.py:27
  164.2 20.7 %all-to-all-start.5 = ((bf16[8,48,1536]{2,1,0:T(8,128)(2,1)}), bf16[8,48,1536]{2,1,0:T(8,128)(2,1)S(1)}, u32[]{:S(2)}, u32[]{:S(2)}) async-start(bf16[8,48,1536]{2,1,0:T(8,128)(2,1)} %broadcast_in_dim.8), calls=%async_computation.5 | async-start | bytes 2359296 | tf_op jit(solution)/shard_map/all_to_all | solution.py:69
  173.3 13.1 %collective-permute-start.5 = (bf16[64,1536]{1,0:T(8,128)(2,1)}, bf16[64,1536]{1,0:T(8,128)(2,1)}, u32[]{:S(2)}, u32[]{:S(2)}) collective-permute-start(bf16[64,1536]{1,0:T(8,128)(2,1)} %get-tuple-element.18), channel_id=1, source_target_pairs={{0,1},{1,0},{2,3},{3,2},{4,5},{5,4},{6,7},{7,6},{8,9},{9,8},{10,11... | collective-permute-start | bytes 589832 | tf_op jit(solution)/shard_map/ppermute | solution.py:31
  173.3 13.6 %collective-permute-start.7 = (bf16[64,1536]{1,0:T(8,128)(2,1)}, bf16[64,1536]{1,0:T(8,128)(2,1)}, u32[]{:S(2)}, u32[]{:S(2)}) collective-permute-start(bf16[64,1536]{1,0:T(8,128)(2,1)} %get-tuple-element.17), channel_id=1, source_target_pairs={{0,1},{1,0},{2,3},{3,2},{4,5},{5,4},{6,7},{7,6},{8,9},{9,8},{10,11... | collective-permute-start | bytes 589832 | tf_op jit(solution)/shard_map/ppermute | solution.py:31
  188.2 9.3 %collective-permute-start.4 = (bf16[64,1536]{1,0:T(8,128)(2,1)S(1)}, bf16[64,1536]{1,0:T(8,128)(2,1)S(1)}, u32[]{:S(2)}, u32[]{:S(2)}) collective-permute-start(bf16[64,1536]{1,0:T(8,128)(2,1)S(1)} %copy-done.21), channel_id=1, source_target_pairs={{0,1},{1,0},{2,3},{3,2},{4,5},{5,4},{6,7},{7,6},{8,9},{9,8},{10,11... | collective-permute-start | bytes 589832 | tf_op jit(solution)/shard_map/ppermute | solution.py:31
  188.7 13.0 %collective-permute-start.8 = (bf16[64,1536]{1,0:T(8,128)(2,1)S(1)}, bf16[64,1536]{1,0:T(8,128)(2,1)S(1)}, u32[]{:S(2)}, u32[]{:S(2)}) collective-permute-start(bf16[64,1536]{1,0:T(8,128)(2,1)S(1)} %get-tuple-element.6), channel_id=1, source_target_pairs={{0,32},{32,64},{64,96},{96,128},{128,160},{160,192},{192,224},{224... | collective-permute-start | bytes 589832 | tf_op jit(solution)/shard_map/ppermute | solution.py:27
  188.7 22.4 %collective-permute-start.6 = (bf16[64,1536]{1,0:T(8,128)(2,1)S(1)}, bf16[64,1536]{1,0:T(8,128)(2,1)S(1)}, u32[]{:S(2)}, u32[]{:S(2)}) collective-permute-start(bf16[64,1536]{1,0:T(8,128)(2,1)S(1)} %get-tuple-element.5), channel_id=1, source_target_pairs={{0,224},{32,0},{64,32},{96,64},{128,96},{160,128},{192,160},{224,1... | collective-permute-start | bytes 589832 | tf_op jit(solution)/shard_map/ppermute | solution.py:27
  192.2 18.9 %collective-permute-start.30 = (bf16[64,1536]{1,0:T(8,128)(2,1)S(1)}, bf16[64,1536]{1,0:T(8,128)(2,1)S(1)}, u32[]{:S(2)}, u32[]{:S(2)}) collective-permute-start(bf16[64,1536]{1,0:T(8,128)(2,1)S(1)} %get-tuple-element.8), channel_id=1, source_target_pairs={{0,128},{32,160},{64,192},{96,224},{128,0},{160,32},{192,64},{224,... | collective-permute-start | bytes 589832 | tf_op jit(solution)/shard_map/ppermute | solution.py:27
  196.5 23.3 %collective-permute-start.28 = (bf16[64,1536]{1,0:T(8,128)(2,1)S(1)}, bf16[64,1536]{1,0:T(8,128)(2,1)S(1)}, u32[]{:S(2)}, u32[]{:S(2)}) collective-permute-start(bf16[64,1536]{1,0:T(8,128)(2,1)S(1)} %get-tuple-element.9), channel_id=1, source_target_pairs={{0,96},{32,128},{64,160},{96,192},{128,224},{160,0},{192,32},{224,... | collective-permute-start | bytes 589832 | tf_op jit(solution)/shard_map/ppermute | solution.py:27
  197.5 22.3 %collective-permute-start.26 = (bf16[64,1536]{1,0:T(8,128)(2,1)S(1)}, bf16[64,1536]{1,0:T(8,128)(2,1)S(1)}, u32[]{:S(2)}, u32[]{:S(2)}) collective-permute-start(bf16[64,1536]{1,0:T(8,128)(2,1)S(1)} %get-tuple-element.7), channel_id=1, source_target_pairs={{0,160},{32,192},{64,224},{96,0},{128,32},{160,64},{192,96},{224,1... | collective-permute-start | bytes 589832 | tf_op jit(solution)/shard_map/ppermute | solution.py:27
  221.0 9.2 %collective-permute-start.31 = (bf16[64,1536]{1,0:T(8,128)(2,1)S(1)}, bf16[64,1536]{1,0:T(8,128)(2,1)S(1)}, u32[]{:S(2)}, u32[]{:S(2)}) collective-permute-start(bf16[64,1536]{1,0:T(8,128)(2,1)S(1)} %get-tuple-element.3), channel_id=1, source_target_pairs={{0,2},{2,0},{1,3},{3,1},{4,6},{6,4},{5,7},{7,5},{8,10},{10,8},{9,1... | collective-permute-start | bytes 589832 | tf_op jit(solution)/shard_map/ppermute | solution.py:31
  (33 other events, 211.6 us)
